TPU v7x, 32 devices: a whole 2x2x4 slice. The times are simulated.
32 devices in a mesh: shot: 4 (over y, x), space: 8 (over z, core).
Axes of the slice: x: 2, y: 2, z: 4, core: 2. Of those that a mesh axis runs over, the one named last changes fastest.
Arguments:
- residual: bfloat16 [4, 2048, 1536], P('shot', 'space'), may hold values from -6 to 6
- record_tile: int32 [4, 2048, 1], P('shot', 'space'), may hold values from 0 to 7; in each aligned block of 256 rows (0 to 255, 256 to 511, ..., all dimensions but the last counted through in order) at most 48 rows name the same one
- record_cell: int32 [4, 2048], P('shot', 'space'), may hold values from 0 to 1023
- time_filter: bfloat16 [6, 1536], replicated, may hold values from -0.15625 to 0.15625
- offsets: int32 [4], P('shot'), may hold values from 0 to 16
- velocity: float32 [4, 64, 128, 256], P('shot', None, 'space'), may hold values from 0.05 to 0.19
- adjoint_prev: float32 [4, 64, 128, 256], P('shot', None, 'space'), may hold values from -6 to 6
- adjoint_now: float32 [4, 64, 128, 256], P('shot', None, 'space'), may hold values from -6 to 6
- forward_accel: bfloat16 [4, 6, 64, 128, 256], P('shot', None, None, 'space'), may hold values from -6 to 6
Outputs:
- gradient: float32 [80, 128, 256], P('shot', 'space')
- adjoint_last: float32 [4, 64, 128, 256], P('shot', None, 'space')
Inputs may be any that keep to these rules, and one draw needn't show every extreme that they name: `record_tile`: among the 256 records of one device, at most 48 name the same tile.
All inputs are finite; a program needn't handle non-finite values.
Results may differ from a plain program's by a relative error of at most 0.0003.
Values sent between devices are 32-bit elements; how exact they have to be, the bound alone decides.
A program may use at most 64 MiB of HBM per device.

v0:
```python
import jax
import jax.numpy as jnp
from jax import lax
from jax.sharding import PartitionSpec as P

STENCIL = (-205.0 / 72.0, 8.0 / 5.0, -1.0 / 5.0, 8.0 / 315.0, -1.0 / 560.0)


def extended(shard, sides, width):
    for axis, dim in sides:
        devices, length = (lax.axis_size(axis), shard.shape[dim])
        up = [(i, (i + 1) % devices) for i in range(devices - 1)]
        down = [(j, i) for i, j in up]
        last = lax.slice_in_dim(shard, length - width, length, axis=dim)
        leading = lax.slice_in_dim(shard, 0, width, axis=dim)
        before = lax.ppermute(last, axis, up)
        after = lax.ppermute(leading, axis, down)
        shard = jnp.concatenate([before, shard, after], axis=dim)
    return shard


def laplace(padded):
    span_y = padded.shape[0] - 8
    span_x = padded.shape[1] - 8
    span_z = padded.shape[2] - 8

    def window(shift_y, shift_x, shift_z):
        return padded[
            4 + shift_y : 4 + shift_y + span_y,
            4 + shift_x : 4 + shift_x + span_x,
            4 + shift_z : 4 + shift_z + span_z,
        ]

    summed = 3.0 * STENCIL[0] * window(0, 0, 0)
    for reach in range(1, 5):
        beside_all = (
            window(reach, 0, 0)
            + window(-reach, 0, 0)
            + window(0, reach, 0)
            + window(0, -reach, 0)
            + window(0, 0, reach)
            + window(0, 0, -reach)
        )
        summed = summed + STENCIL[reach] * beside_all
    return summed


def pad_sides(field):
    return jnp.pad(field, ((4, 4), (0, 0), (4, 4)))


def local(
    residual,
    record_tile,
    record_cell,
    time_filter,
    offsets,
    velocity,
    adjoint_prev,
    adjoint_now,
    forward_accel,
):
    tiles_count = lax.axis_size("space")
    record_count = residual.shape[1]
    cells_y = velocity.shape[1]
    cells_x = velocity.shape[2]
    step_count = forward_accel.shape[1]
    slot_count = record_count * 3 // 16
    surface = cells_y * cells_x
    block_rows = (cells_y + cells_y // 4) // lax.axis_size("shot")
    trace_rows = residual[0]
    tile_ids = record_tile[0, :, 0]
    cell_ids = record_cell[0]
    one_hot = (tile_ids[:, None] == jnp.arange(tiles_count, dtype=jnp.int32)[None, :]).astype(
        jnp.int32
    )
    order_rank = jnp.sum((jnp.cumsum(one_hot, axis=0) - 1) * one_hot, axis=1)
    slot_index = tile_ids * slot_count + order_rank
    cell_buffer = (
        jnp.full((tiles_count * slot_count,), surface, jnp.int32).at[slot_index].set(cell_ids)
    )
    cell_buffer = cell_buffer.reshape(tiles_count, slot_count)
    filtered = jnp.dot(trace_rows, time_filter.T, preferred_element_type=jnp.float32)
    value_buffer = (
        jnp.zeros((tiles_count * slot_count, step_count), jnp.float32).at[slot_index].set(filtered)
    )
    value_buffer = value_buffer.reshape(tiles_count, slot_count, step_count)
    values, arrived_cells = (
        lax.all_to_all(value_buffer, "space", split_axis=0, concat_axis=0, tiled=True),
        lax.all_to_all(cell_buffer, "space", split_axis=0, concat_axis=0, tiled=True),
    )
    source = jax.ops.segment_sum(
        values.reshape(-1, step_count), arrived_cells.reshape(-1), num_segments=surface + 1
    )[:surface]
    source = source.T.reshape(step_count, cells_y, cells_x)
    shift_rows = offsets[0]
    speed_sq = velocity[0]
    previous = adjoint_prev[0]
    current = adjoint_now[0]
    forward = forward_accel[0]
    imaging = jnp.zeros_like(current)
    for moment in range(step_count):
        rimmed = extended(current, (("space", 1),), 4)
        advanced = 2.0 * current - previous + speed_sq * laplace(pad_sides(rimmed))
        advanced = advanced.at[:, :, 0].add(source[moment])
        imaging = imaging + forward[moment] * advanced
        previous, current = (current, advanced)
    row_index = jnp.arange(lax.axis_size("shot") * block_rows, dtype=jnp.int32) - shift_rows
    inside = (row_index >= 0) & (row_index < cells_y)
    chosen = jnp.take(imaging, jnp.clip(row_index, 0, cells_y - 1), axis=0)
    gradient = lax.psum_scatter(
        jnp.where(inside[:, None, None], chosen, 0.0), "shot", scatter_dimension=0, tiled=True
    )
    return (gradient, current[None])


def solution(mesh):
    in_specs = (
        P("shot", "space", None),
        P("shot", "space", None),
        P("shot", "space"),
        P(),
        P("shot"),
        P("shot", None, "space", None),
        P("shot", None, "space", None),
        P("shot", None, "space", None),
        P("shot", None, None, "space", None),
    )
    out_specs = (P("shot", "space", None), P("shot", None, "space", None))
    return jax.shard_map(local, mesh=mesh, in_specs=in_specs, out_specs=out_specs, check_vma=False)
```

profile of v0, /device:TPU:0, one launch (start us, length us, event | category | flops | bytes accessed | tf_op | source)
XLA Modules:
  0.0 252.7 jit_solution(15057840573693914089)
XLA Ops:
  12.5 6.3 %all-to-all-start = ((s32[8,1,48]{2,1,0:T(1,128)}), s32[8,1,48]{2,1,0:T(1,128)S(1)}, u32[]{:S(2)}, u32[]{:S(2)}) async-start(s32[8,1,48]{2,1,0:T(1,128)} %all_to_all.9), calls=%async_computation | async-start | bytes 8192 | tf_op jit(solution)/shard_map/all_to_all | solution.py:90
  21.9 2.4 all-to-all-done
  24.3 3.3 %all-to-all-start.1 = ((f32[8,1,288]{2,1,0:T(1,128)}), f32[8,1,288]{2,1,0:T(1,128)S(1)}, u32[]{:S(2)}, u32[]{:S(2)}) async-start(f32[8,1,288]{2,1,0:T(1,128)} %reshape.372), calls=%async_computation.1 | async-start | bytes 24576 | tf_op jit(solution)/shard_map/all_to_all | solution.py:89
  29.0 2.3 collective-permute-start
  35.2 2.7 %scatter_custom_fusion.2 = f32[1025,6]{1,0:T(8,128)S(1)} fusion(s32[384]{0:T(512)S(1)} %reshape.349, f32[384,6]{1,0:T(8,128)S(1)} %bitcast.79, f32[]{:T(128)} %constant.167.clone.1), kind=kCustom, calls=%fused_computation.345 | custom fusion | flops 2304 | bytes 24604 | tf_op jit(solution)/shard_map/scatter-add | solution.py:92
  38.0 2.4 fusion.205
  41.1 2.2 select_maximum_fusion.10
  43.3 11.4 %fusion.146 = f32[64,16,256]{2,1,0:T(8,128)} fusion(f32[64,16,256]{2,1,0:T(8,128)} %bitcast.69, f32[64,4,256]{2,1,0:T(4,128)} %copy-done.4, f32[64,4,256]{2,1,0:T(4,128)} %collective-permute-done.1, f32[72,24,264]{2,1,0:T(8,128)S(1)} %select_maximum_fusion.10, f32[1,64,16,256]{3,2,1,0:T(8,128)} %param.26, f32[1,64,16,256]{3,2,1,0:T(8,128)} %param.27), kind=kLoop, calls=%fused_computation.239 | loop fusion | flops 10747904 | bytes 21495808 | tf_op jit(solution)/shard_map/add | solution.py:104
  56.0 2.4 scatter-add.29
  59.7 3.4 %collective-permute-start.2 = (f32[64,4,256]{2,1,0:T(4,128)S(1)}, f32[64,4,256]{2,1,0:T(4,128)S(1)}, u32[]{:S(2)}, u32[]{:S(2)}) collective-permute-start(f32[64,4,256]{2,1,0:T(4,128)S(1)} %get-tuple-element.85), channel_id=1, source_target_pairs={{0,1},{1,2},{2,3},{3,4},{4,5},{5,6},{6,7},{8,9},{9,10},{10,11},{11... | collective-permute-start | bytes 786440 | tf_op jit(solution)/shard_map/ppermute | solution.py:16
  64.6 3.1 %collective-permute-done.3 = f32[64,4,256]{2,1,0:T(4,128)S(1)} collective-permute-done((f32[64,4,256]{2,1,0:T(4,128)S(1)}, f32[64,4,256]{2,1,0:T(4,128)S(1)}, u32[]{:S(2)}, u32[]{:S(2)}) %collective-permute-start.3) | collective-permute-done | bytes 262176 | tf_op jit(solution)/shard_map/ppermute | solution.py:17
  68.4 2.4 select_maximum_fusion.8
  70.9 11.2 %fusion.119 = f32[64,16,256]{2,1,0:T(8,128)} fusion(f32[64,16,256]{2,1,0:T(8,128)} %scatter-add.29, f32[64,4,256]{2,1,0:T(4,128)} %copy-done.8, f32[64,4,256]{2,1,0:T(4,128)} %copy-done.12, f32[72,24,264]{2,1,0:T(8,128)S(1)} %select_maximum_fusion.8, f32[1,64,16,256]{3,2,1,0:T(8,128)} %param.26, f32[1,64,16,256]{3,2,1,0:T(8,128)} %param.28), kind=kLoop, calls=%fused_computation.212 | loop fusion | flops 10747904 | bytes 21495808 | tf_op jit(solution)/shard_map/add | solution.py:104
  83.3 2.4 scatter-add.30
  87.1 6.7 %collective-permute-start.4 = (f32[64,4,256]{2,1,0:T(4,128)S(1)}, f32[64,4,256]{2,1,0:T(4,128)S(1)}, u32[]{:S(2)}, u32[]{:S(2)}) collective-permute-start(f32[64,4,256]{2,1,0:T(4,128)S(1)} %get-tuple-element.83), channel_id=1, source_target_pairs={{0,1},{1,2},{2,3},{3,4},{4,5},{5,6},{6,7},{8,9},{9,10},{10,11},{11... | collective-permute-start | bytes 786440 | tf_op jit(solution)/shard_map/ppermute | solution.py:16
  97.9 2.4 select_maximum_fusion.6
  100.3 12.0 %fusion.92 = f32[64,16,256]{2,1,0:T(8,128)} fusion(f32[64,16,256]{2,1,0:T(8,128)} %scatter-add.30, f32[64,4,256]{2,1,0:T(4,128)} %copy-done.9, f32[64,4,256]{2,1,0:T(4,128)} %copy-done.13, f32[72,24,264]{2,1,0:T(8,128)S(1)} %select_maximum_fusion.6, f32[1,64,16,256]{3,2,1,0:T(8,128)} %param.26, f32[64,16,256]{2,1,0:T(8,128)} %scatter-add.29), kind=kLoop, calls=%fused_computation.185 | loop fusion | flops 10747904 | bytes 21495808 | tf_op jit(solution)/shard_map/add | solution.py:104
  113.6 2.4 scatter-add.31
  117.3 6.5 %collective-permute-start.6 = (f32[64,4,256]{2,1,0:T(4,128)S(1)}, f32[64,4,256]{2,1,0:T(4,128)S(1)}, u32[]{:S(2)}, u32[]{:S(2)}) collective-permute-start(f32[64,4,256]{2,1,0:T(4,128)S(1)} %get-tuple-element.81), channel_id=1, source_target_pairs={{0,1},{1,2},{2,3},{3,4},{4,5},{5,6},{6,7},{8,9},{9,10},{10,11},{11... | collective-permute-start | bytes 786440 | tf_op jit(solution)/shard_map/ppermute | solution.py:16
  128.0 2.4 select_maximum_fusion.4
  130.4 11.7 %fusion.65 = f32[64,16,256]{2,1,0:T(8,128)} fusion(f32[64,16,256]{2,1,0:T(8,128)} %scatter-add.31, f32[64,4,256]{2,1,0:T(4,128)} %copy-done.10, f32[64,4,256]{2,1,0:T(4,128)} %copy-done.14, f32[72,24,264]{2,1,0:T(8,128)S(1)} %select_maximum_fusion.4, f32[1,64,16,256]{3,2,1,0:T(8,128)} %param.26, f32[64,16,256]{2,1,0:T(8,128)} %scatter-add.30), kind=kLoop, calls=%fused_computation.158 | loop fusion | flops 10747904 | bytes 21495808 | tf_op jit(solution)/shard_map/add | solution.py:104
  143.4 2.4 scatter-add.34
  147.1 6.2 %collective-permute-start.8 = (f32[64,4,256]{2,1,0:T(4,128)S(1)}, f32[64,4,256]{2,1,0:T(4,128)S(1)}, u32[]{:S(2)}, u32[]{:S(2)}) collective-permute-start(f32[64,4,256]{2,1,0:T(4,128)S(1)} %get-tuple-element.79), channel_id=1, source_target_pairs={{0,1},{1,2},{2,3},{3,4},{4,5},{5,6},{6,7},{8,9},{9,10},{10,11},{11... | collective-permute-start | bytes 786440 | tf_op jit(solution)/shard_map/ppermute | solution.py:16
  157.5 2.4 select_maximum_fusion.2
  159.9 11.1 %fusion.38 = f32[64,16,256]{2,1,0:T(8,128)} fusion(f32[64,16,256]{2,1,0:T(8,128)} %scatter-add.34, f32[64,4,256]{2,1,0:T(4,128)} %copy-done.7, f32[64,4,256]{2,1,0:T(4,128)} %copy-done.11, f32[72,24,264]{2,1,0:T(8,128)S(1)} %select_maximum_fusion.2, f32[1,64,16,256]{3,2,1,0:T(8,128)} %param.26, f32[64,16,256]{2,1,0:T(8,128)} %scatter-add.31), kind=kLoop, calls=%fused_computation.131 | loop fusion | flops 10747904 | bytes 21495808 | tf_op jit(solution)/shard_map/add | solution.py:104
  172.3 2.4 scatter-add.42
  176.1 6.2 %collective-permute-start.10 = (f32[64,4,256]{2,1,0:T(4,128)S(1)}, f32[64,4,256]{2,1,0:T(4,128)S(1)}, u32[]{:S(2)}, u32[]{:S(2)}) collective-permute-start(f32[64,4,256]{2,1,0:T(4,128)S(1)} %get-tuple-element.77), channel_id=1, source_target_pairs={{0,1},{1,2},{2,3},{3,4},{4,5},{5,6},{6,7},{8,9},{9,10},{10,11},{11... | collective-permute-start | bytes 786440 | tf_op jit(solution)/shard_map/ppermute | solution.py:16
  186.4 2.4 select_maximum_fusion
  188.8 11.2 %fusion.11 = f32[64,16,256]{2,1,0:T(8,128)} fusion(f32[64,16,256]{2,1,0:T(8,128)} %scatter-add.42, f32[64,4,256]{2,1,0:T(4,128)} %copy-done.5, f32[64,4,256]{2,1,0:T(4,128)} %copy-done.6, f32[72,24,264]{2,1,0:T(8,128)S(1)} %select_maximum_fusion, f32[1,64,16,256]{3,2,1,0:T(8,128)} %param.26, f32[64,16,256]{2,1,0:T(8,128)} %scatter-add.34), kind=kLoop, calls=%fused_computation.104 | loop fusion | flops 10747904 | bytes 21495808 | tf_op jit(solution)/shard_map/add | solution.py:104
  201.5 2.4 scatter-add.43
  203.9 5.1 %fusion.183 = f32[64,16,256]{2,1,0:T(8,128)} fusion(f32[64,16,256]{2,1,0:T(8,128)} %scatter-add.43, f32[64,16,256]{2,1,0:T(8,128)} %scatter-add.42, f32[64,16,256]{2,1,0:T(8,128)} %scatter-add.34, f32[64,16,256]{2,1,0:T(8,128)} %scatter-add.31, f32[64,16,256]{2,1,0:T(8,128)S(1)} %copy-done.2, f32[64,16,256]{2,1,0:T(8,128)S(1)} %copy-done.1, ...), kind=kLoop, calls=%fused_computation.325 | loop fusion | flops 4456448 | bytes 10485760 | tf_op jit(solution)/shard_map/add | solution.py:106
  212.2 33.7 %reduce-scatter.2.cloned.1.call-done = f32[20,16,256]{2,1,0:T(8,128)} async-done(((f32[80,16,256]{2,1,0:T(8,128)}), f32[20,16,256]{2,1,0:T(8,128)}) %reduce-scatter.2.cloned.1.call-update) | async-done | bytes 327696 | tf_op jit(solution)/shard_map/reduce_scatter | solution.py:111
  (88 shorter events, 49.8 us)
Async XLA Ops:
  7.2 11.6 %copy-start = (bf16[1,256,1536]{2,1,0:T(8,128)(2,1)S(1)}, bf16[1,256,1536]{2,1,0:T(8,128)(2,1)}, u32[]{:S(2)}) copy-start(bf16[1,256,1536]{2,1,0:T(8,128)(2,1)} %param.21) | copy-start | bytes 2359300
  12.5 11.8 %all-to-all-start = ((s32[8,1,48]{2,1,0:T(1,128)}), s32[8,1,48]{2,1,0:T(1,128)S(1)}, u32[]{:S(2)}, u32[]{:S(2)}) async-start(s32[8,1,48]{2,1,0:T(1,128)} %all_to_all.9), calls=%async_computation | async-start | bytes 8192 | tf_op jit(solution)/shard_map/all_to_all | solution.py:90
  24.3 9.5 %all-to-all-start.1 = ((f32[8,1,288]{2,1,0:T(1,128)}), f32[8,1,288]{2,1,0:T(1,128)S(1)}, u32[]{:S(2)}, u32[]{:S(2)}) async-start(f32[8,1,288]{2,1,0:T(1,128)} %reshape.372), calls=%async_computation.1 | async-start | bytes 24576 | tf_op jit(solution)/shard_map/all_to_all | solution.py:89
  27.6 218.3 %reduce-scatter.2.cloned.1.call-start = ((), (), s32[]{:S(2)}) async-start(), calls=%async_computation.3 | async-start | bytes 1638400 | tf_op jit(solution)/shard_map/reduce_scatter | solution.py:111
  29.0 11.4 %collective-permute-start = (f32[64,4,256]{2,1,0:T(4,128)S(1)}, f32[64,4,256]{2,1,0:T(4,128)S(1)}, u32[]{:S(2)}, u32[]{:S(2)}) collective-permute-start(f32[64,4,256]{2,1,0:T(4,128)S(1)} %get-tuple-element.87), channel_id=1, source_target_pairs={{0,1},{1,2},{2,3},{3,4},{4,5},{5,6},{6,7},{8,9},{9,10},{10,11},{11... | collective-permute-start | bytes 786440 | tf_op jit(solution)/shard_map/ppermute | solution.py:16
  31.2 9.8 %collective-permute-start.1 = (f32[64,4,256]{2,1,0:T(4,128)S(1)}, f32[64,4,256]{2,1,0:T(4,128)}, u32[]{:S(2)}, u32[]{:S(2)}) collective-permute-start(f32[64,4,256]{2,1,0:T(4,128)S(1)} %get-tuple-element.86), channel_id=1, source_target_pairs={{1,0},{2,1},{3,2},{4,3},{5,4},{6,5},{7,6},{9,8},{10,9},{11,10},{12... | collective-permute-start | bytes 786440 | tf_op jit(solution)/shard_map/ppermute | solution.py:17
  38.0 3.1 %copy-start.3 = (f32[1,64,16,256]{3,2,1,0:T(8,128)S(1)}, f32[1,64,16,256]{3,2,1,0:T(8,128)}, u32[]{:S(2)}) copy-start(f32[1,64,16,256]{3,2,1,0:T(8,128)} %param.28) | copy-start | bytes 3145732
  40.4 0.7 copy-start.4
  59.7 4.9 %collective-permute-start.2 = (f32[64,4,256]{2,1,0:T(4,128)S(1)}, f32[64,4,256]{2,1,0:T(4,128)S(1)}, u32[]{:S(2)}, u32[]{:S(2)}) collective-permute-start(f32[64,4,256]{2,1,0:T(4,128)S(1)} %get-tuple-element.85), channel_id=1, source_target_pairs={{0,1},{1,2},{2,3},{3,4},{4,5},{5,6},{6,7},{8,9},{9,10},{10,11},{11... | collective-permute-start | bytes 786440 | tf_op jit(solution)/shard_map/ppermute | solution.py:16
  63.1 4.6 %collective-permute-start.3 = (f32[64,4,256]{2,1,0:T(4,128)S(1)}, f32[64,4,256]{2,1,0:T(4,128)S(1)}, u32[]{:S(2)}, u32[]{:S(2)}) collective-permute-start(f32[64,4,256]{2,1,0:T(4,128)S(1)} %get-tuple-element.84), channel_id=1, source_target_pairs={{1,0},{2,1},{3,2},{4,3},{5,4},{6,5},{7,6},{9,8},{10,9},{11,10},{12... | collective-permute-start | bytes 786440 | tf_op jit(solution)/shard_map/ppermute | solution.py:17
  64.6 3.1 %copy-start.8 = (f32[64,4,256]{2,1,0:T(4,128)}, f32[64,4,256]{2,1,0:T(4,128)S(1)}, u32[]{:S(2)}) copy-start(f32[64,4,256]{2,1,0:T(4,128)S(1)} %collective-permute-done.2) | copy-start | bytes 786436
  67.7 0.7 copy-start.12
  87.1 8.0 %collective-permute-start.4 = (f32[64,4,256]{2,1,0:T(4,128)S(1)}, f32[64,4,256]{2,1,0:T(4,128)S(1)}, u32[]{:S(2)}, u32[]{:S(2)}) collective-permute-start(f32[64,4,256]{2,1,0:T(4,128)S(1)} %get-tuple-element.83), channel_id=1, source_target_pairs={{0,1},{1,2},{2,3},{3,4},{4,5},{5,6},{6,7},{8,9},{9,10},{10,11},{11... | collective-permute-start | bytes 786440 | tf_op jit(solution)/shard_map/ppermute | solution.py:16
  93.7 3.4 %collective-permute-start.5 = (f32[64,4,256]{2,1,0:T(4,128)S(1)}, f32[64,4,256]{2,1,0:T(4,128)S(1)}, u32[]{:S(2)}, u32[]{:S(2)}) collective-permute-start(f32[64,4,256]{2,1,0:T(4,128)S(1)} %get-tuple-element.82), channel_id=1, source_target_pairs={{1,0},{2,1},{3,2},{4,3},{5,4},{6,5},{7,6},{9,8},{10,9},{11,10},{12... | collective-permute-start | bytes 786440 | tf_op jit(solution)/shard_map/ppermute | solution.py:17
  95.0 2.1 copy-start.9
  97.2 0.7 copy-start.13
  117.3 8.0 %collective-permute-start.6 = (f32[64,4,256]{2,1,0:T(4,128)S(1)}, f32[64,4,256]{2,1,0:T(4,128)S(1)}, u32[]{:S(2)}, u32[]{:S(2)}) collective-permute-start(f32[64,4,256]{2,1,0:T(4,128)S(1)} %get-tuple-element.81), channel_id=1, source_target_pairs={{0,1},{1,2},{2,3},{3,4},{4,5},{5,6},{6,7},{8,9},{9,10},{10,11},{11... | collective-permute-start | bytes 786440 | tf_op jit(solution)/shard_map/ppermute | solution.py:16
  123.8 3.4 %collective-permute-start.7 = (f32[64,4,256]{2,1,0:T(4,128)S(1)}, f32[64,4,256]{2,1,0:T(4,128)S(1)}, u32[]{:S(2)}, u32[]{:S(2)}) collective-permute-start(f32[64,4,256]{2,1,0:T(4,128)S(1)} %get-tuple-element.80), channel_id=1, source_target_pairs={{1,0},{2,1},{3,2},{4,3},{5,4},{6,5},{7,6},{9,8},{10,9},{11,10},{12... | collective-permute-start | bytes 786440 | tf_op jit(solution)/shard_map/ppermute | solution.py:17
  125.3 1.9 copy-start.10
  127.2 0.7 copy-start.14
  147.1 8.2 %collective-permute-start.8 = (f32[64,4,256]{2,1,0:T(4,128)S(1)}, f32[64,4,256]{2,1,0:T(4,128)S(1)}, u32[]{:S(2)}, u32[]{:S(2)}) collective-permute-start(f32[64,4,256]{2,1,0:T(4,128)S(1)} %get-tuple-element.79), channel_id=1, source_target_pairs={{0,1},{1,2},{2,3},{3,4},{4,5},{5,6},{6,7},{8,9},{9,10},{10,11},{11... | collective-permute-start | bytes 786440 | tf_op jit(solution)/shard_map/ppermute | solution.py:16
  153.4 3.4 %collective-permute-start.9 = (f32[64,4,256]{2,1,0:T(4,128)S(1)}, f32[64,4,256]{2,1,0:T(4,128)S(1)}, u32[]{:S(2)}, u32[]{:S(2)}) collective-permute-start(f32[64,4,256]{2,1,0:T(4,128)S(1)} %get-tuple-element.78), channel_id=1, source_target_pairs={{1,0},{2,1},{3,2},{4,3},{5,4},{6,5},{7,6},{9,8},{10,9},{11,10},{12... | collective-permute-start | bytes 786440 | tf_op jit(solution)/shard_map/ppermute | solution.py:17
  155.3 1.5 copy-start.7
  156.8 0.7 copy-start.11
  176.1 7.8 %collective-permute-start.10 = (f32[64,4,256]{2,1,0:T(4,128)S(1)}, f32[64,4,256]{2,1,0:T(4,128)S(1)}, u32[]{:S(2)}, u32[]{:S(2)}) collective-permute-start(f32[64,4,256]{2,1,0:T(4,128)S(1)} %get-tuple-element.77), channel_id=1, source_target_pairs={{0,1},{1,2},{2,3},{3,4},{4,5},{5,6},{6,7},{8,9},{9,10},{10,11},{11... | collective-permute-start | bytes 786440 | tf_op jit(solution)/shard_map/ppermute | solution.py:16
  182.2 3.4 %collective-permute-start.11 = (f32[64,4,256]{2,1,0:T(4,128)S(1)}, f32[64,4,256]{2,1,0:T(4,128)S(1)}, u32[]{:S(2)}, u32[]{:S(2)}) collective-permute-start(f32[64,4,256]{2,1,0:T(4,128)S(1)} %get-tuple-element.76), channel_id=1, source_target_pairs={{1,0},{2,1},{3,2},{4,3},{5,4},{6,5},{7,6},{9,8},{10,9},{11,10},{12... | collective-permute-start | bytes 786440 | tf_op jit(solution)/shard_map/ppermute | solution.py:17
  183.9 1.8 copy-start.5
  185.7 0.7 copy-start.6
  200.1 3.8 %copy-start.1 = (f32[64,16,256]{2,1,0:T(8,128)S(1)}, f32[64,16,256]{2,1,0:T(8,128)}, u32[]{:S(2)}) copy-start(f32[64,16,256]{2,1,0:T(8,128)} %scatter-add.29) | copy-start | bytes 3145732
  200.1 3.8 %copy-start.2 = (f32[64,16,256]{2,1,0:T(8,128)S(1)}, f32[64,16,256]{2,1,0:T(8,128)}, u32[]{:S(2)}) copy-start(f32[64,16,256]{2,1,0:T(8,128)} %scatter-add.30) | copy-start | bytes 3145732
Sparse Core Ops, SparseCore 0:
  212.3 33.5 reduce-scatter.1
where the time goes:
time: 254 us; the launch traced here: 253 us
  other arithmetic  104 us (41%)
  starting transfers between devices  49.4 us (19%)
  waiting for transfers between devices  46.5 us (18%)
  local copies, waits for them, and re-layouts  36.5 us (14%)
  between operations  15.1 us (6%)
    add x6, other arithmetic, local(): advanced = 2.0 * current - previous + speed_sq * laplace(pad_sides(rimmed))  68.7 us
    reduce_scatter x1, waiting for transfers between devices, local(): lax.psum_scatter(jnp.where(inside[:, None, None], chosen, 0.0), 'shot', s...  33.7 us
    ppermute x6, starting transfers between devices, extended(): before = lax.ppermute(last, axis, up)  31.3 us
    scatter-add x6, local copies, waits for them, and re-layouts, local(): advanced = advanced.at[:, :, 0].add(source[moment])  14.4 us
    concatenate x6, other arithmetic, extended(): shard = jnp.concatenate([before, shard, after], axis=dim)  14.4 us
    ppermute x6, waiting for transfers between devices, extended(): after = lax.ppermute(leading, axis, down)  10.4 us
    ppermute x6, starting transfers between devices, extended(): after = lax.ppermute(leading, axis, down)  8.41 us
    add x6, other arithmetic, local(): advanced = advanced.at[:, :, 0].add(source[moment])  7.76 us
  transfers between devices with their start and end apart: 15, of which 7 were waited for; matrix products, arithmetic and copies ran while one was open for 5% of the time, Pallas kernels for 0%

commit v1 on v0

v1 whole, which is shorter than its diff:
```python
import functools

import jax
import jax.numpy as jnp
import numpy as np
from jax import lax
from jax.experimental import pallas as pl
from jax.experimental.pallas import tpu as pltpu
from jax.sharding import PartitionSpec as P

STENCIL = (-205.0 / 72.0, 8.0 / 5.0, -1.0 / 5.0, 8.0 / 315.0, -1.0 / 560.0)
MESH = pl.DeviceIdType.MESH
F32 = jnp.float32
BF16 = jnp.bfloat16
CX = 16
CHUNK_Y = 16
ROWS = CHUNK_Y * CX
EDGE = CHUNK_Y * 4
PAD = 64


def pieces(matrix):
    high = np.asarray(matrix, np.float32).astype(jnp.bfloat16)
    low = (matrix - high.astype(np.float64)).astype(np.float32).astype(jnp.bfloat16)
    return high, low


def coefficient(distance):
    distance = abs(distance)
    return STENCIL[distance] if 1 <= distance <= 4 else 0.0


def matrices(depth):
    along_z = np.zeros((depth, depth))
    for i in range(depth):
        along_z[i, i] = 3.0 * STENCIL[0]
        for j in range(max(0, i - 4), min(depth, i + 5)):
            if i != j:
                along_z[j, i] = coefficient(i - j)
    across = np.zeros((8 * CX, 16 * CX))
    for y in range(8):
        for x in range(CX):
            for other in range(16):
                across[y * CX + x, other * CX + x] += coefficient(other - 4 - y)
            for other in range(CX):
                across[y * CX + x, (y + 4) * CX + other] += coefficient(other - x)
    rim = np.zeros((ROWS, 2 * EDGE))
    for y in range(CHUNK_Y):
        for x in range(CX):
            for j in range(4):
                rim[y * CX + x, y * 4 + j] = coefficient(x + 4 - j)
                rim[y * CX + x, EDGE + y * 4 + j] = coefficient(16 + j - x)
    z_high, z_low = pieces(along_z)
    a_high, a_low = pieces(across)
    r_high, r_low = pieces(rim)
    return (
        z_high,
        z_low,
        np.concatenate([a_high, a_low], axis=0),
        np.concatenate([r_high, r_high], axis=1),
        r_low,
    )


def split(value):
    high = value.astype(BF16)
    low = (value - high.astype(F32)).astype(BF16)
    return high, low


def dot(a, b):
    return jnp.dot(a, b, preferred_element_type=F32)


def dot_nt(a, b):
    return lax.dot_general(a, b, (((1,), (1,)), ((), ())), preferred_element_type=F32)


def kernel(
    spaces,
    shots,
    steps,
    residual,
    codes,
    time_filter,
    offsets,
    z_high,
    z_low,
    across,
    rim_high,
    rim_low,
    now_hbm,
    previous_hbm,
    velocity_hbm,
    forward_hbm,
    gradient,
    last_hbm,
    q,
    high,
    low,
    speed,
    forward,
    image,
    source,
    gathered,
    halo_out,
    halo_in,
    stack_out,
    stack_in,
    local_sem,
    gather_send,
    gather_recv,
    halo_send,
    halo_recv,
    stack_send,
    stack_recv,
):
    cells = q.shape[1]
    chunks = cells // ROWS
    depth = q.shape[2]
    band = gradient.shape[0]
    lead = cells // CX // 4
    shot = lax.axis_index("shot")
    me = lax.axis_index("space")

    loads = [
        pltpu.make_async_copy(now_hbm, q.at[0], local_sem.at[0]),
        pltpu.make_async_copy(previous_hbm, q.at[1], local_sem.at[1]),
        pltpu.make_async_copy(velocity_hbm, speed, local_sem.at[2]),
        pltpu.make_async_copy(forward_hbm, forward, local_sem.at[3]),
    ]
    for load in loads:
        load.start()

    barrier = pltpu.get_barrier_semaphore()
    for d in range(1, spaces):
        pl.semaphore_signal(
            barrier, inc=1, device_id=(shot, lax.rem(me + d, spaces)), device_id_type=MESH
        )
    for d in range(1, shots):
        pl.semaphore_signal(
            barrier, inc=1, device_id=(lax.rem(shot + d, shots), me), device_id_type=MESH
        )

    gathered[me, 0:8, :] = jnp.zeros((8, gathered.shape[2]), F32)
    gathered[me, 0:steps, :] = dot_nt(time_filter[...], residual[...])
    gathered[me, 6:7, :] = codes[...]

    for slot in range(2):
        for piece in (high, low):
            piece[slot, 0:PAD, :] = jnp.zeros((PAD, depth), BF16)
            piece[slot, PAD + cells :, :] = jnp.zeros((PAD, depth), BF16)
    image[...] = jnp.zeros(image.shape, F32)

    has_left = me > 0
    has_right = me < spaces - 1

    @pl.when(jnp.logical_not(has_left))
    def _():
        halo_in[:, 0] = jnp.zeros((2,) + halo_in.shape[2:], F32)

    @pl.when(jnp.logical_not(has_right))
    def _():
        halo_in[:, 1] = jnp.zeros((2,) + halo_in.shape[2:], F32)

    pl.semaphore_wait(barrier, spaces - 1 + shots - 1)

    def gather_copy(d):
        return pltpu.make_async_remote_copy(
            src_ref=gathered.at[me],
            dst_ref=gathered.at[me],
            send_sem=gather_send.at[d - 1],
            recv_sem=gather_recv.at[d - 1],
            device_id=(shot, lax.rem(me + d, spaces)),
            device_id_type=MESH,
        )

    def gather_arrival(d):
        owner = lax.rem(me + spaces - d, spaces)
        return pltpu.make_async_remote_copy(
            src_ref=gathered.at[owner],
            dst_ref=gathered.at[owner],
            send_sem=gather_send.at[d - 1],
            recv_sem=gather_recv.at[d - 1],
            device_id=(shot, lax.rem(me + d, spaces)),
            device_id_type=MESH,
        )

    def halo_copy(slot, side, c):
        target = me - 1 if side == 0 else me + 1
        rows = pl.ds(c * EDGE, EDGE)
        return pltpu.make_async_remote_copy(
            src_ref=halo_out.at[slot, side, rows],
            dst_ref=halo_in.at[slot, 1 - side, rows],
            send_sem=halo_send.at[slot, side, c],
            recv_sem=halo_recv.at[slot, 1 - side, c],
            device_id=(shot, target),
            device_id_type=MESH,
        )

    def halo_arrival(slot, side, c):
        target = me - 1 if side == 0 else me + 1
        rows = pl.ds(c * EDGE, EDGE)
        return pltpu.make_async_remote_copy(
            src_ref=halo_out.at[slot, side, rows],
            dst_ref=halo_in.at[slot, side, rows],
            send_sem=halo_send.at[slot, side, c],
            recv_sem=halo_recv.at[slot, side, c],
            device_id=(shot, target),
            device_id_type=MESH,
        )

    first_half = lax.broadcasted_iota(jnp.int32, (8, depth), 0) < 4

    def publish_edges(slot, c, value):
        for pair in range(CHUNK_Y // 2):
            base = pair * 2 * CX
            low_a = value[base : base + 8]
            high_a = value[base + 8 : base + 16]
            low_b = value[base + 16 : base + 24]
            high_b = value[base + 24 : base + 32]
            at = pl.ds(c * EDGE + pair * 8, 8)
            halo_out[slot, 0, at, :] = jnp.where(first_half, low_a, pltpu.roll(low_b, 4, 0))
            halo_out[slot, 1, at, :] = jnp.where(first_half, pltpu.roll(high_a, 4, 0), high_b)

        @pl.when(has_left)
        def _():
            halo_copy(slot, 0, c).start()

        @pl.when(has_right)
        def _():
            halo_copy(slot, 1, c).start()

    def wait_edges_sent(slot, c):
        @pl.when(has_left)
        def _():
            halo_copy(slot, 0, c).wait_send()

        @pl.when(has_right)
        def _():
            halo_copy(slot, 1, c).wait_send()

    def publish_pieces(slot, c, value):
        value_high, value_low = split(value)
        high[slot, pl.ds(PAD + c * ROWS, ROWS), :] = value_high
        low[slot, pl.ds(PAD + c * ROWS, ROWS), :] = value_low

    for d in range(1, spaces):
        gather_copy(d).start()
    loads[0].wait()
    for c in range(chunks):
        publish_edges(0, c, q[0, pl.ds(c * ROWS, ROWS), :])
    for c in range(chunks):
        publish_pieces(0, c, q[0, pl.ds(c * ROWS, ROWS), :])

    for d in range(1, spaces):
        gather_arrival(d).wait_recv()
    first_cell = (me * cells).astype(F32)

    def add_block(j, totals):
        block = gathered[j]
        block_high = block.astype(BF16).astype(F32)
        stacked = jnp.concatenate(
            [block_high, block - block_high, jnp.zeros((112, block.shape[1]), F32)], axis=0
        ).astype(BF16)
        wanted = block[6:7, :] - first_cell
        for c in range(chunks):
            cell = (lax.broadcasted_iota(jnp.int32, (ROWS, block.shape[1]), 0) + c * ROWS).astype(F32)
            hot = jnp.where(wanted == cell, 1.0, 0.0).astype(BF16)
            source[pl.ds(c * ROWS, ROWS), :] += dot_nt(hot, stacked)
        return totals

    source[...] = jnp.zeros(source.shape, F32)
    lax.fori_loop(0, spaces, add_block, 0)
    source[...] = source[...] + pltpu.roll(source[...], 120, 1)

    for load in loads[1:]:
        load.wait()

    first_lane = lax.broadcasted_iota(jnp.int32, (ROWS, 128), 1) == 0

    def step(k, carry):
        slot = lax.rem(k, 2)
        other = 1 - slot
        for c in range(chunks):
            rows = pl.ds(c * ROWS, ROWS)
            mid_high = high[slot, pl.ds(PAD + c * ROWS, ROWS), :]
            mid_low = low[slot, pl.ds(PAD + c * ROWS, ROWS), :]
            spread = dot(mid_high, z_high[...]) + dot(mid_high, z_low[...])
            spread = spread + dot(mid_low, z_high[...])
            parts = []
            for sub in range(2):
                window = pl.ds((2 * c + sub) * 128, 256)
                both = dot(across[...], high[slot, window, :])
                parts.append(both[:128] + both[128:] + dot(across[0:128], low[slot, window, :]))
            spread = spread + jnp.concatenate(parts, axis=0)

            @pl.when(has_left)
            def _():
                halo_arrival(slot, 0, c).wait_recv()

            @pl.when(has_right)
            def _():
                halo_arrival(slot, 1, c).wait_recv()

            at = pl.ds(c * EDGE, EDGE)
            rim = jnp.concatenate([halo_in[slot, 0, at, :], halo_in[slot, 1, at, :]], axis=0)
            rim_h, rim_l = split(rim)
            spread = spread + dot(rim_high[...], jnp.concatenate([rim_h, rim_l], axis=0))
            spread = spread + dot(rim_low[...], rim_h)

            value = 2.0 * q[slot, rows, :] - q[other, rows, :] + speed[rows, :] * spread
            added = source[rows, :]
            first = value[:, :128] + jnp.where(first_lane, added, 0.0)
            source[rows, :] = pltpu.roll(added, 127, 1)
            value = jnp.concatenate([first, value[:, 128:]], axis=1)
            q[other, rows, :] = value

            @pl.when(k < steps - 1)
            def _():
                @pl.when(k >= 1)
                def _():
                    wait_edges_sent(other, c)

                publish_edges(other, c, value)
                publish_pieces(other, c, value)

            inside = pl.ds(lead + c * CHUNK_Y, CHUNK_Y)
            product = forward[k, rows, :].astype(F32) * value
            image[inside] += product.reshape(CHUNK_Y, CX, depth)
        return carry

    lax.fori_loop(0, steps, step, 0)
    result = pltpu.make_async_copy(q.at[steps % 2], last_hbm, local_sem.at[0])
    result.start()

    moved = offsets[0]
    band_y = band // CX

    def shift_into(place, owner):
        for y in range(band_y):
            place[pl.ds(y * CX, CX), :] = image[owner * band_y + y - moved + lead]

    copies = []
    for d in range(1, shots):
        target = lax.rem(shot + d, shots)
        shift_into(stack_out.at[d - 1], target)
        copy = pltpu.make_async_remote_copy(
            src_ref=stack_out.at[d - 1],
            dst_ref=stack_in.at[d - 1],
            send_sem=stack_send.at[d - 1],
            recv_sem=stack_recv.at[d - 1],
            device_id=(target, me),
            device_id_type=MESH,
        )
        copy.start()
        copies.append(copy)
    shift_into(gradient, shot)
    for d in range(1, spaces):
        gather_copy(d).wait_send()
    for slot in range(2):
        for c in range(chunks):
            wait_edges_sent(slot, c)
    for d, copy in enumerate(copies):
        copy.wait_recv()
        gradient[...] += stack_in[d]
    for copy in copies:
        copy.wait_send()
    result.wait()


def local(
    spaces,
    shots,
    residual,
    record_tile,
    record_cell,
    time_filter,
    offsets,
    velocity,
    adjoint_prev,
    adjoint_now,
    forward_accel,
):
    _, ny, cx, depth = velocity.shape
    steps = forward_accel.shape[1]
    cells = ny * cx
    records = residual.shape[1]
    grid_y = ny + ny // 4
    band = grid_y // shots * cx
    chunks = cells // ROWS
    codes = (record_tile[0, :, 0] * cells + record_cell[0]).astype(F32)[None]
    constants = [jnp.asarray(matrix) for matrix in matrices(depth)]
    vmem = pl.BlockSpec(memory_space=pltpu.VMEM)
    anywhere = pl.BlockSpec(memory_space=pl.ANY)
    gradient, last = pl.pallas_call(
        functools.partial(kernel, spaces, shots, steps),
        out_shape=(
            jax.ShapeDtypeStruct((band, depth), F32),
            jax.ShapeDtypeStruct((cells, depth), F32),
        ),
        in_specs=[vmem] * 3
        + [pl.BlockSpec(memory_space=pltpu.SMEM)]
        + [vmem] * 5
        + [anywhere] * 4,
        out_specs=(vmem, anywhere),
        scratch_shapes=[
            pltpu.VMEM((2, cells, depth), F32),
            pltpu.VMEM((2, cells + 2 * PAD, depth), BF16),
            pltpu.VMEM((2, cells + 2 * PAD, depth), BF16),
            pltpu.VMEM((cells, depth), F32),
            pltpu.VMEM((steps, cells, depth), BF16),
            pltpu.VMEM((ny + 2 * (ny // 4), cx, depth), F32),
            pltpu.VMEM((cells, 128), F32),
            pltpu.VMEM((spaces, 8, records), F32),
            pltpu.VMEM((2, 2, chunks * EDGE, depth), F32),
            pltpu.VMEM((2, 2, chunks * EDGE, depth), F32),
            pltpu.VMEM((shots - 1, band, depth), F32),
            pltpu.VMEM((shots - 1, band, depth), F32),
            pltpu.SemaphoreType.DMA((4,)),
            pltpu.SemaphoreType.DMA((spaces - 1,)),
            pltpu.SemaphoreType.DMA((spaces - 1,)),
            pltpu.SemaphoreType.DMA((2, 2, chunks)),
            pltpu.SemaphoreType.DMA((2, 2, chunks)),
            pltpu.SemaphoreType.DMA((shots - 1,)),
            pltpu.SemaphoreType.DMA((shots - 1,)),
        ],
        compiler_params=pltpu.CompilerParams(
            collective_id=0, has_side_effects=True, vmem_limit_bytes=44 * 1024 * 1024
        ),
        cost_estimate=pl.CostEstimate(flops=6 * 10**9, bytes_accessed=8 * 10**6, transcendentals=0),
    )(
        residual[0],
        codes,
        time_filter,
        offsets,
        *constants,
        adjoint_now.reshape(cells, depth),
        adjoint_prev.reshape(cells, depth),
        velocity.reshape(cells, depth),
        forward_accel.reshape(steps, cells, depth),
    )
    return gradient.reshape(grid_y // shots, cx, depth), last.reshape(1, ny, cx, depth)


def solution(mesh):
    in_specs = (
        P("shot", "space", None),
        P("shot", "space", None),
        P("shot", "space"),
        P(),
        P("shot"),
        P("shot", None, "space", None),
        P("shot", None, "space", None),
        P("shot", None, "space", None),
        P("shot", None, None, "space", None),
    )
    out_specs = (P("shot", "space", None), P("shot", None, "space", None))
    body = functools.partial(local, mesh.shape["space"], mesh.shape["shot"])
    return jax.shard_map(body, mesh=mesh, in_specs=in_specs, out_specs=out_specs, check_vma=False)
```

time: 254 us -> 65.4 us (0.26)
  other arithmetic: 104 us -> 0.7 us
  starting transfers between devices: 49.4 us -> 0 us
  Pallas kernels: 0 us -> 49.3 us
  waiting for transfers between devices: 46.5 us -> 0 us
  local copies, waits for them, and re-layouts: 36.5 us -> 13.6 us
  between operations: 15.1 us -> 1.3 us
    add x13 -> x0, other arithmetic: 81.5 us -> none  [the longest x6 68.7 us: local(): advanced = 2.0 * current - previous + speed_sq * laplace(pad_sides(rimmed))]
    pallas_call x0 -> x1, Pallas kernels: none -> 49.3 us  [local(): pl.pallas_call(functools.partial(kernel, spaces, shots, steps), out_shape...]
    ppermute x12 -> x0, starting transfers between devices: 39.7 us -> none  [the longest x6 31.3 us: extended(): before = lax.ppermute(last, axis, up)]
    reduce_scatter x1 -> x0, waiting for transfers between devices: 33.7 us -> none  [local(): lax.psum_scatter(jnp.where(inside[:, None, None], chosen, 0.0), 'shot', s...]
    scatter-add x6 -> x0, local copies, waits for them, and re-layouts: 14.4 us -> none  [local(): advanced = advanced.at[:, :, 0].add(source[moment])]
    concatenate x6 -> x0, other arithmetic: 14.4 us -> none  [extended(): shard = jnp.concatenate([before, shard, after], axis=dim)]
    ppermute x12 -> x0, waiting for transfers between devices: 10.4 us -> none  [the longest x6 10.4 us: extended(): after = lax.ppermute(leading, axis, down)]
    slice x7 -> x0, local copies, waits for them, and re-layouts: 10.1 us -> none  [the longest x6 7.75 us: extended(): leading = lax.slice_in_dim(shard, 0, width, axis=dim)]
  transfers between devices with their start and end apart: 15 -> 0, of which waited for: 7 -> 0; matrix products, arithmetic and copies ran while one was open for 5% -> 0% of each run, Pallas kernels for 0% -> 0%
where the time goes in v1:
time: 65.4 us; the launch traced here: 64.8 us
  Pallas kernels  49.3 us (75%)
  local copies, waits for them, and re-layouts  13.6 us (21%)
  between operations  1.3 us (2%)
  other arithmetic  0.7 us (1%)
    pallas_call x1, Pallas kernels, local(): pl.pallas_call(functools.partial(kernel, spaces, shots, steps), out_shape...  49.3 us
    unnamed x24, local copies, waits for them, and re-layouts  13.6 us

profile of v1, /device:TPU:0, one launch (start us, length us, event | category | flops | bytes accessed | tf_op | source)
XLA Modules:
  0.0 64.8 jit_solution(9006366585371611168)
XLA Ops:
  1.3 0.7 %fusion.codes = f32[1,256]{1,0:T(1,128)S(1)} fusion(s32[1,256]{1,0:T(1,128)} %param.16, s32[1,256,1]{1,2,0:T(1,128)} %param.15), kind=kLoop, calls=%fused_computation.1 | loop fusion | flops 768 | bytes 3072 | tf_op jit(solution)/shard_map/convert_element_type | solution.py:392
  2.0 0.0 copy-start
  2.0 1.9 %copy-done = bf16[1,6,64,16,256]{4,3,2,1,0:T(8,128)(2,1)S(1)} copy-done((bf16[1,6,64,16,256]{4,3,2,1,0:T(8,128)(2,1)S(1)}, bf16[1,6,64,16,256]{4,3,2,1,0:T(8,128)(2,1)}, u32[]{:S(2)}) %copy-start) | copy-done | bytes 3145752
  3.9 0.0 copy-start.1
  3.9 1.2 %copy-done.1 = f32[1,64,16,256]{3,2,1,0:T(8,128)S(1)} copy-done((f32[1,64,16,256]{3,2,1,0:T(8,128)S(1)}, f32[1,64,16,256]{3,2,1,0:T(8,128)}, u32[]{:S(2)}) %copy-start.1) | copy-done | bytes 1048600
  5.1 0.0 copy-start.2
  5.1 1.2 %copy-done.2 = f32[1,64,16,256]{3,2,1,0:T(8,128)S(1)} copy-done((f32[1,64,16,256]{3,2,1,0:T(8,128)S(1)}, f32[1,64,16,256]{3,2,1,0:T(8,128)}, u32[]{:S(2)}) %copy-start.2) | copy-done | bytes 1048600
  6.3 0.0 copy-start.3
  6.3 1.2 %copy-done.3 = f32[1,64,16,256]{3,2,1,0:T(8,128)S(1)} copy-done((f32[1,64,16,256]{3,2,1,0:T(8,128)S(1)}, f32[1,64,16,256]{3,2,1,0:T(8,128)}, u32[]{:S(2)}) %copy-start.3) | copy-done | bytes 1048600
  7.5 0.0 copy-start.4
  7.5 1.1 %copy-done.4 = bf16[1,256,1536]{2,1,0:T(8,128)(2,1)S(1)} copy-done((bf16[1,256,1536]{2,1,0:T(8,128)(2,1)S(1)}, bf16[1,256,1536]{2,1,0:T(8,128)(2,1)}, u32[]{:S(2)}) %copy-start.4) | copy-done | bytes 786456
  8.7 0.0 copy-start.5
  8.7 0.7 %copy-done.5 = bf16[6,1536]{1,0:T(8,128)(2,1)S(1)} copy-done((bf16[6,1536]{1,0:T(8,128)(2,1)S(1)}, bf16[6,1536]{1,0:T(8,128)(2,1)}, u32[]{:S(2)}) %copy-start.5) | copy-done | bytes 18456
  9.4 0.0 copy-start.6
  9.4 0.9 %copy-done.6 = bf16[256,256]{1,0:T(8,128)(2,1)S(1)} copy-done((bf16[256,256]{1,0:T(8,128)(2,1)S(1)}, bf16[256,256]{1,0:T(8,128)(2,1)}, u32[]{:S(2)}) %copy-start.6) | copy-done | bytes 131096
  10.3 0.0 copy-start.7
  10.3 0.9 %copy-done.7 = bf16[256,256]{1,0:T(8,128)(2,1)S(1)} copy-done((bf16[256,256]{1,0:T(8,128)(2,1)S(1)}, bf16[256,256]{1,0:T(8,128)(2,1)}, u32[]{:S(2)}) %copy-start.7) | copy-done | bytes 131096
  11.2 0.0 copy-start.8
  11.2 0.9 %copy-done.8 = bf16[256,256]{1,0:T(8,128)(2,1)S(1)} copy-done((bf16[256,256]{1,0:T(8,128)(2,1)S(1)}, bf16[256,256]{1,0:T(8,128)(2,1)}, u32[]{:S(2)}) %copy-start.8) | copy-done | bytes 131096
  12.1 0.0 copy-start.9
  12.1 0.9 %copy-done.9 = bf16[256,256]{1,0:T(8,128)(2,1)S(1)} copy-done((bf16[256,256]{1,0:T(8,128)(2,1)S(1)}, bf16[256,256]{1,0:T(8,128)(2,1)}, u32[]{:S(2)}) %copy-start.9) | copy-done | bytes 131096
  13.0 0.0 copy-start.10
  13.0 0.8 %copy-done.10 = bf16[256,128]{1,0:T(8,128)(2,1)S(1)} copy-done((bf16[256,128]{1,0:T(8,128)(2,1)S(1)}, bf16[256,128]{1,0:T(8,128)(2,1)}, u32[]{:S(2)}) %copy-start.10) | copy-done | bytes 65560
  13.9 49.3 %shard_map.149 = (f32[320,256]{1,0:T(8,128)S(1)}, f32[1024,256]{1,0:T(8,128)S(1)}) custom-call(bf16[256,1536]{1,0:T(8,128)(2,1)S(1)} %bitcast.17, f32[1,256]{1,0:T(1,128)S(1)} %fusion.codes, bf16[6,1536]{1,0:T(8,128)(2,1)S(1)} %copy-done.5, s32[1]{0:T(128)S(6)} %copy.18.offsets, bf16[256,256]{1,0:T(8,128)(2,1)S(1)} %copy-done.9, ...), custom_call_target="tpu_custom_call" | custom-call | flops 6000000000 | bytes 8000000 | tf_op jit(solution)/shard_map/pallas_call | solution.py:396
  63.1 0.7 %copy.19 = f32[20,16,256]{2,1,0:T(8,128)} copy(f32[20,16,256]{2,1,0:T(8,128)S(1)} %bitcast.12) | data formatting | bytes 655360
  63.9 1.0 %copy.20 = f32[1,64,16,256]{3,2,1,0:T(8,128)} copy(f32[1,64,16,256]{3,2,1,0:T(8,128)S(1)} %bitcast.11) | data formatting | bytes 2097152
Async XLA Ops:
  2.0 1.9 %copy-start = (bf16[1,6,64,16,256]{4,3,2,1,0:T(8,128)(2,1)S(1)}, bf16[1,6,64,16,256]{4,3,2,1,0:T(8,128)(2,1)}, u32[]{:S(2)}) copy-start(bf16[1,6,64,16,256]{4,3,2,1,0:T(8,128)(2,1)} %param.22) | copy-start | bytes 9437188
  3.9 1.2 %copy-start.1 = (f32[1,64,16,256]{3,2,1,0:T(8,128)S(1)}, f32[1,64,16,256]{3,2,1,0:T(8,128)}, u32[]{:S(2)}) copy-start(f32[1,64,16,256]{3,2,1,0:T(8,128)} %param.21) | copy-start | bytes 3145732
  5.1 1.2 %copy-start.2 = (f32[1,64,16,256]{3,2,1,0:T(8,128)S(1)}, f32[1,64,16,256]{3,2,1,0:T(8,128)}, u32[]{:S(2)}) copy-start(f32[1,64,16,256]{3,2,1,0:T(8,128)} %param.20) | copy-start | bytes 3145732
  6.3 1.2 %copy-start.3 = (f32[1,64,16,256]{3,2,1,0:T(8,128)S(1)}, f32[1,64,16,256]{3,2,1,0:T(8,128)}, u32[]{:S(2)}) copy-start(f32[1,64,16,256]{3,2,1,0:T(8,128)} %param.19) | copy-start | bytes 3145732
  7.5 1.1 %copy-start.4 = (bf16[1,256,1536]{2,1,0:T(8,128)(2,1)S(1)}, bf16[1,256,1536]{2,1,0:T(8,128)(2,1)}, u32[]{:S(2)}) copy-start(bf16[1,256,1536]{2,1,0:T(8,128)(2,1)} %param.14) | copy-start | bytes 2359300
  8.7 0.7 %copy-start.5 = (bf16[6,1536]{1,0:T(8,128)(2,1)S(1)}, bf16[6,1536]{1,0:T(8,128)(2,1)}, u32[]{:S(2)}) copy-start(bf16[6,1536]{1,0:T(8,128)(2,1)} %time_filter.1) | copy-start | bytes 55300
  9.4 0.9 %copy-start.6 = (bf16[256,256]{1,0:T(8,128)(2,1)S(1)}, bf16[256,256]{1,0:T(8,128)(2,1)}, u32[]{:S(2)}) copy-start(bf16[256,256]{1,0:T(8,128)(2,1)} %constant.15.clone.rim_high) | copy-start | bytes 393220
  10.3 0.9 %copy-start.7 = (bf16[256,256]{1,0:T(8,128)(2,1)S(1)}, bf16[256,256]{1,0:T(8,128)(2,1)}, u32[]{:S(2)}) copy-start(bf16[256,256]{1,0:T(8,128)(2,1)} %constant.14.clone.across) | copy-start | bytes 393220
  11.2 0.9 %copy-start.8 = (bf16[256,256]{1,0:T(8,128)(2,1)S(1)}, bf16[256,256]{1,0:T(8,128)(2,1)}, u32[]{:S(2)}) copy-start(bf16[256,256]{1,0:T(8,128)(2,1)} %constant.13.clone.z_low) | copy-start | bytes 393220
  12.1 0.9 %copy-start.9 = (bf16[256,256]{1,0:T(8,128)(2,1)S(1)}, bf16[256,256]{1,0:T(8,128)(2,1)}, u32[]{:S(2)}) copy-start(bf16[256,256]{1,0:T(8,128)(2,1)} %constant.12.clone.z_high) | copy-start | bytes 393220
  13.0 0.8 %copy-start.10 = (bf16[256,128]{1,0:T(8,128)(2,1)S(1)}, bf16[256,128]{1,0:T(8,128)(2,1)}, u32[]{:S(2)}) copy-start(bf16[256,128]{1,0:T(8,128)(2,1)} %constant.16.clone.rim_low) | copy-start | bytes 196612

commit v2 on v1

--- a/solution.py
+++ b/solution.py
@@ -80,21 +80,28 @@
     spaces,
     shots,
     steps,
-    residual,
+    residual_hbm,
     codes,
-    time_filter,
+    filter_hbm,
     offsets,
-    z_high,
-    z_low,
-    across,
-    rim_high,
-    rim_low,
+    z_high_hbm,
+    z_low_hbm,
+    across_hbm,
+    rim_high_hbm,
+    rim_low_hbm,
     now_hbm,
     previous_hbm,
     velocity_hbm,
     forward_hbm,
     gradient,
     last_hbm,
+    residual,
+    time_filter,
+    z_high,
+    z_low,
+    across,
+    rim_high,
+    rim_low,
     q,
     high,
     low,
@@ -123,11 +130,21 @@
     shot = lax.axis_index("shot")
     me = lax.axis_index("space")
 
+    pairs = (
+        (now_hbm, q.at[0]),
+        (residual_hbm, residual),
+        (filter_hbm, time_filter),
+        (z_high_hbm, z_high),
+        (z_low_hbm, z_low),
+        (across_hbm, across),
+        (rim_high_hbm, rim_high),
+        (rim_low_hbm, rim_low),
+        (previous_hbm, q.at[1]),
+        (velocity_hbm, speed),
+        (forward_hbm, forward),
+    )
     loads = [
-        pltpu.make_async_copy(now_hbm, q.at[0], local_sem.at[0]),
-        pltpu.make_async_copy(previous_hbm, q.at[1], local_sem.at[1]),
-        pltpu.make_async_copy(velocity_hbm, speed, local_sem.at[2]),
-        pltpu.make_async_copy(forward_hbm, forward, local_sem.at[3]),
+        pltpu.make_async_copy(there, here, local_sem.at[i]) for i, (there, here) in enumerate(pairs)
     ]
     for load in loads:
         load.start()
@@ -141,10 +158,6 @@
         pl.semaphore_signal(
             barrier, inc=1, device_id=(lax.rem(shot + d, shots), me), device_id_type=MESH
         )
-
-    gathered[me, 0:8, :] = jnp.zeros((8, gathered.shape[2]), F32)
-    gathered[me, 0:steps, :] = dot_nt(time_filter[...], residual[...])
-    gathered[me, 6:7, :] = codes[...]
 
     for slot in range(2):
         for piece in (high, low):
@@ -245,11 +258,16 @@
         high[slot, pl.ds(PAD + c * ROWS, ROWS), :] = value_high
         low[slot, pl.ds(PAD + c * ROWS, ROWS), :] = value_low
 
-    for d in range(1, spaces):
-        gather_copy(d).start()
     loads[0].wait()
     for c in range(chunks):
         publish_edges(0, c, q[0, pl.ds(c * ROWS, ROWS), :])
+    loads[1].wait()
+    loads[2].wait()
+    gathered[me, 0:8, :] = jnp.zeros((8, gathered.shape[2]), F32)
+    gathered[me, 0:steps, :] = dot_nt(time_filter[...], residual[...])
+    gathered[me, 6:7, :] = codes[...]
+    for d in range(1, spaces):
+        gather_copy(d).start()
     for c in range(chunks):
         publish_pieces(0, c, q[0, pl.ds(c * ROWS, ROWS), :])
 
@@ -274,7 +292,7 @@
     lax.fori_loop(0, spaces, add_block, 0)
     source[...] = source[...] + pltpu.roll(source[...], 120, 1)
 
-    for load in loads[1:]:
+    for load in loads[3:]:
         load.wait()
 
     first_lane = lax.broadcasted_iota(jnp.int32, (ROWS, 128), 1) == 0
@@ -392,19 +410,19 @@
     codes = (record_tile[0, :, 0] * cells + record_cell[0]).astype(F32)[None]
     constants = [jnp.asarray(matrix) for matrix in matrices(depth)]
     vmem = pl.BlockSpec(memory_space=pltpu.VMEM)
-    anywhere = pl.BlockSpec(memory_space=pl.ANY)
+    there = pl.BlockSpec(memory_space=pltpu.HBM)
     gradient, last = pl.pallas_call(
         functools.partial(kernel, spaces, shots, steps),
         out_shape=(
             jax.ShapeDtypeStruct((band, depth), F32),
             jax.ShapeDtypeStruct((cells, depth), F32),
         ),
-        in_specs=[vmem] * 3
-        + [pl.BlockSpec(memory_space=pltpu.SMEM)]
-        + [vmem] * 5
-        + [anywhere] * 4,
-        out_specs=(vmem, anywhere),
+        in_specs=[there, vmem, there, pl.BlockSpec(memory_space=pltpu.SMEM)] + [there] * 9,
+        out_specs=(vmem, pl.BlockSpec(memory_space=pl.ANY)),
         scratch_shapes=[
+            pltpu.VMEM((records, residual.shape[2]), BF16),
+            pltpu.VMEM(time_filter.shape, BF16),
+            *[pltpu.VMEM(matrix.shape, BF16) for matrix in constants],
             pltpu.VMEM((2, cells, depth), F32),
             pltpu.VMEM((2, cells + 2 * PAD, depth), BF16),
             pltpu.VMEM((2, cells + 2 * PAD, depth), BF16),
@@ -417,7 +435,7 @@
             pltpu.VMEM((2, 2, chunks * EDGE, depth), F32),
             pltpu.VMEM((shots - 1, band, depth), F32),
             pltpu.VMEM((shots - 1, band, depth), F32),
-            pltpu.SemaphoreType.DMA((4,)),
+            pltpu.SemaphoreType.DMA((11,)),
             pltpu.SemaphoreType.DMA((spaces - 1,)),
             pltpu.SemaphoreType.DMA((spaces - 1,)),
             pltpu.SemaphoreType.DMA((2, 2, chunks)),

time: 65.4 us -> 69 us (1.055)
  Pallas kernels: 49.3 us -> 52.9 us
    pallas_call x1, Pallas kernels: 49.3 us -> 52.9 us  [local(): pl.pallas_call(functools.partial(kernel, spaces, shots, steps), out_shape...]
where the time goes in v2:
time: 69 us; the launch traced here: 68.5 us
  Pallas kernels  52.9 us (77%)
  local copies, waits for them, and re-layouts  13.6 us (20%)
  between operations  1.3 us (2%)
  other arithmetic  0.7 us (1%)
    pallas_call x1, Pallas kernels, local(): pl.pallas_call(functools.partial(kernel, spaces, shots, steps), out_shape...  52.9 us
    unnamed x24, local copies, waits for them, and re-layouts  13.6 us

profile of v2, /device:TPU:0, one launch (start us, length us, event | category | flops | bytes accessed | tf_op | source)
XLA Modules:
  0.0 68.5 jit_solution(17593649570303579884)
XLA Ops:
  1.3 0.7 %fusion.codes = f32[1,256]{1,0:T(1,128)S(1)} fusion(s32[1,256]{1,0:T(1,128)} %param.16, s32[1,256,1]{1,2,0:T(1,128)} %param.15), kind=kLoop, calls=%fused_computation.1 | loop fusion | flops 768 | bytes 3072 | tf_op jit(solution)/shard_map/convert_element_type | solution.py:410
  2.0 0.0 copy-start
  2.0 1.9 %copy-done = bf16[1,6,64,16,256]{4,3,2,1,0:T(8,128)(2,1)S(1)} copy-done((bf16[1,6,64,16,256]{4,3,2,1,0:T(8,128)(2,1)S(1)}, bf16[1,6,64,16,256]{4,3,2,1,0:T(8,128)(2,1)}, u32[]{:S(2)}) %copy-start) | copy-done | bytes 3145752
  3.9 0.0 copy-start.1
  3.9 1.2 %copy-done.1 = f32[1,64,16,256]{3,2,1,0:T(8,128)S(1)} copy-done((f32[1,64,16,256]{3,2,1,0:T(8,128)S(1)}, f32[1,64,16,256]{3,2,1,0:T(8,128)}, u32[]{:S(2)}) %copy-start.1) | copy-done | bytes 1048600
  5.1 0.0 copy-start.2
  5.1 1.2 %copy-done.2 = f32[1,64,16,256]{3,2,1,0:T(8,128)S(1)} copy-done((f32[1,64,16,256]{3,2,1,0:T(8,128)S(1)}, f32[1,64,16,256]{3,2,1,0:T(8,128)}, u32[]{:S(2)}) %copy-start.2) | copy-done | bytes 1048600
  6.3 0.0 copy-start.3
  6.3 1.2 %copy-done.3 = f32[1,64,16,256]{3,2,1,0:T(8,128)S(1)} copy-done((f32[1,64,16,256]{3,2,1,0:T(8,128)S(1)}, f32[1,64,16,256]{3,2,1,0:T(8,128)}, u32[]{:S(2)}) %copy-start.3) | copy-done | bytes 1048600
  7.5 0.0 copy-start.4
  7.5 1.1 %copy-done.4 = bf16[1,256,1536]{2,1,0:T(8,128)(2,1)S(1)} copy-done((bf16[1,256,1536]{2,1,0:T(8,128)(2,1)S(1)}, bf16[1,256,1536]{2,1,0:T(8,128)(2,1)}, u32[]{:S(2)}) %copy-start.4) | copy-done | bytes 786456
  8.7 0.0 copy-start.5
  8.7 0.7 %copy-done.5 = bf16[6,1536]{1,0:T(8,128)(2,1)S(1)} copy-done((bf16[6,1536]{1,0:T(8,128)(2,1)S(1)}, bf16[6,1536]{1,0:T(8,128)(2,1)}, u32[]{:S(2)}) %copy-start.5) | copy-done | bytes 18456
  9.4 0.0 copy-start.6
  9.4 0.9 %copy-done.6 = bf16[256,256]{1,0:T(8,128)(2,1)S(1)} copy-done((bf16[256,256]{1,0:T(8,128)(2,1)S(1)}, bf16[256,256]{1,0:T(8,128)(2,1)}, u32[]{:S(2)}) %copy-start.6) | copy-done | bytes 131096
  10.3 0.0 copy-start.7
  10.3 0.9 %copy-done.7 = bf16[256,256]{1,0:T(8,128)(2,1)S(1)} copy-done((bf16[256,256]{1,0:T(8,128)(2,1)S(1)}, bf16[256,256]{1,0:T(8,128)(2,1)}, u32[]{:S(2)}) %copy-start.7) | copy-done | bytes 131096
  11.2 0.0 copy-start.8
  11.2 0.9 %copy-done.8 = bf16[256,256]{1,0:T(8,128)(2,1)S(1)} copy-done((bf16[256,256]{1,0:T(8,128)(2,1)S(1)}, bf16[256,256]{1,0:T(8,128)(2,1)}, u32[]{:S(2)}) %copy-start.8) | copy-done | bytes 131096
  12.1 0.0 copy-start.9
  12.1 0.9 %copy-done.9 = bf16[256,256]{1,0:T(8,128)(2,1)S(1)} copy-done((bf16[256,256]{1,0:T(8,128)(2,1)S(1)}, bf16[256,256]{1,0:T(8,128)(2,1)}, u32[]{:S(2)}) %copy-start.9) | copy-done | bytes 131096
  13.0 0.0 copy-start.10
  13.0 0.8 %copy-done.10 = bf16[256,128]{1,0:T(8,128)(2,1)S(1)} copy-done((bf16[256,128]{1,0:T(8,128)(2,1)S(1)}, bf16[256,128]{1,0:T(8,128)(2,1)}, u32[]{:S(2)}) %copy-start.10) | copy-done | bytes 65560
  13.9 52.9 %shard_map.149 = (f32[320,256]{1,0:T(8,128)S(1)}, f32[1024,256]{1,0:T(8,128)S(1)}) custom-call(bf16[256,1536]{1,0:T(8,128)(2,1)S(1)} %bitcast.17, f32[1,256]{1,0:T(1,128)S(1)} %fusion.codes, bf16[6,1536]{1,0:T(8,128)(2,1)S(1)} %copy-done.5, s32[1]{0:T(128)S(6)} %copy.18.offsets, bf16[256,256]{1,0:T(8,128)(2,1)S(1)} %copy-done.9, ...), custom_call_target="tpu_custom_call" | custom-call | flops 6000000000 | bytes 8000000 | tf_op jit(solution)/shard_map/pallas_call | solution.py:414
  66.8 0.7 %copy.19 = f32[20,16,256]{2,1,0:T(8,128)} copy(f32[20,16,256]{2,1,0:T(8,128)S(1)} %bitcast.12) | data formatting | bytes 655360
  67.5 1.0 %copy.20 = f32[1,64,16,256]{3,2,1,0:T(8,128)} copy(f32[1,64,16,256]{3,2,1,0:T(8,128)S(1)} %bitcast.11) | data formatting | bytes 2097152
Async XLA Ops:
  2.0 1.9 %copy-start = (bf16[1,6,64,16,256]{4,3,2,1,0:T(8,128)(2,1)S(1)}, bf16[1,6,64,16,256]{4,3,2,1,0:T(8,128)(2,1)}, u32[]{:S(2)}) copy-start(bf16[1,6,64,16,256]{4,3,2,1,0:T(8,128)(2,1)} %param.22) | copy-start | bytes 9437188
  3.9 1.2 %copy-start.1 = (f32[1,64,16,256]{3,2,1,0:T(8,128)S(1)}, f32[1,64,16,256]{3,2,1,0:T(8,128)}, u32[]{:S(2)}) copy-start(f32[1,64,16,256]{3,2,1,0:T(8,128)} %param.21) | copy-start | bytes 3145732
  5.1 1.2 %copy-start.2 = (f32[1,64,16,256]{3,2,1,0:T(8,128)S(1)}, f32[1,64,16,256]{3,2,1,0:T(8,128)}, u32[]{:S(2)}) copy-start(f32[1,64,16,256]{3,2,1,0:T(8,128)} %param.20) | copy-start | bytes 3145732
  6.3 1.2 %copy-start.3 = (f32[1,64,16,256]{3,2,1,0:T(8,128)S(1)}, f32[1,64,16,256]{3,2,1,0:T(8,128)}, u32[]{:S(2)}) copy-start(f32[1,64,16,256]{3,2,1,0:T(8,128)} %param.19) | copy-start | bytes 3145732
  7.5 1.1 %copy-start.4 = (bf16[1,256,1536]{2,1,0:T(8,128)(2,1)S(1)}, bf16[1,256,1536]{2,1,0:T(8,128)(2,1)}, u32[]{:S(2)}) copy-start(bf16[1,256,1536]{2,1,0:T(8,128)(2,1)} %param.14) | copy-start | bytes 2359300
  8.7 0.7 %copy-start.5 = (bf16[6,1536]{1,0:T(8,128)(2,1)S(1)}, bf16[6,1536]{1,0:T(8,128)(2,1)}, u32[]{:S(2)}) copy-start(bf16[6,1536]{1,0:T(8,128)(2,1)} %filter_hbm.1) | copy-start | bytes 55300
  9.4 0.9 %copy-start.6 = (bf16[256,256]{1,0:T(8,128)(2,1)S(1)}, bf16[256,256]{1,0:T(8,128)(2,1)}, u32[]{:S(2)}) copy-start(bf16[256,256]{1,0:T(8,128)(2,1)} %constant.15.clone.rim_high_hbm) | copy-start | bytes 393220
  10.3 0.9 %copy-start.7 = (bf16[256,256]{1,0:T(8,128)(2,1)S(1)}, bf16[256,256]{1,0:T(8,128)(2,1)}, u32[]{:S(2)}) copy-start(bf16[256,256]{1,0:T(8,128)(2,1)} %constant.14.clone.across_hbm) | copy-start | bytes 393220
  11.2 0.9 %copy-start.8 = (bf16[256,256]{1,0:T(8,128)(2,1)S(1)}, bf16[256,256]{1,0:T(8,128)(2,1)}, u32[]{:S(2)}) copy-start(bf16[256,256]{1,0:T(8,128)(2,1)} %constant.13.clone.z_low_hbm) | copy-start | bytes 393220
  12.1 0.9 %copy-start.9 = (bf16[256,256]{1,0:T(8,128)(2,1)S(1)}, bf16[256,256]{1,0:T(8,128)(2,1)}, u32[]{:S(2)}) copy-start(bf16[256,256]{1,0:T(8,128)(2,1)} %constant.12.clone.z_high_hbm) | copy-start | bytes 393220
  13.0 0.8 %copy-start.10 = (bf16[256,128]{1,0:T(8,128)(2,1)S(1)}, bf16[256,128]{1,0:T(8,128)(2,1)}, u32[]{:S(2)}) copy-start(bf16[256,128]{1,0:T(8,128)(2,1)} %constant.16.clone.rim_low_hbm) | copy-start | bytes 196612

commit v3 on v2

--- a/solution.py
+++ b/solution.py
@@ -444,7 +444,7 @@
             pltpu.SemaphoreType.DMA((shots - 1,)),
         ],
         compiler_params=pltpu.CompilerParams(
-            collective_id=0, has_side_effects=True, vmem_limit_bytes=44 * 1024 * 1024
+            collective_id=0, has_side_effects=True, vmem_limit_bytes=60 * 1024 * 1024
         ),
         cost_estimate=pl.CostEstimate(flops=6 * 10**9, bytes_accessed=8 * 10**6, transcendentals=0),
     )(

time: 69 us -> 59.7 us (0.87)
  local copies, waits for them, and re-layouts: 13.6 us -> 3.98 us
    unnamed x24 -> x2, local copies, waits for them, and re-layouts: 13.6 us -> 3.98 us
where the time goes in v3:
time: 59.7 us; the launch traced here: 59.5 us
  Pallas kernels  53 us (89%)
  local copies, waits for them, and re-layouts  3.98 us (7%)
  between operations  1.29 us (2%)
  other arithmetic  1.26 us (2%)
    pallas_call x1, Pallas kernels, local(): pl.pallas_call(functools.partial(kernel, spaces, shots, steps), out_shape...  53 us
    unnamed x2, local copies, waits for them, and re-layouts  3.98 us
    convert_element_type x1, other arithmetic, local(): codes = (record_tile[0, :, 0] * cells + record_cell[0]).astype(F32)[None]  1.26 us

profile of v3, /device:TPU:0, one launch (start us, length us, event | category | flops | bytes accessed | tf_op | source)
XLA Modules:
  0.0 59.5 jit_solution(10036227894838774353)
XLA Ops:
  1.3 1.3 %fusion.codes = f32[1,256]{1,0:T(1,128)} fusion(s32[1,256]{1,0:T(1,128)} %param.16, s32[1,256,1]{1,2,0:T(1,128)} %param.15), kind=kLoop, calls=%fused_computation.1 | loop fusion | flops 768 | bytes 3072 | tf_op jit(solution)/shard_map/convert_element_type | solution.py:410
  2.5 53.0 %shard_map.149 = (f32[320,256]{1,0:T(8,128)}, f32[1024,256]{1,0:T(8,128)}) custom-call(bf16[256,1536]{1,0:T(8,128)(2,1)} %bitcast.17, f32[1,256]{1,0:T(1,128)} %fusion.codes, bf16[6,1536]{1,0:T(8,128)(2,1)} %filter_hbm.1, s32[1]{0:T(128)S(6)} %copy.18.offsets, bf16[256,256]{1,0:T(8,128)(2,1)} %constant.12.clone.z_high_hbm, ...), custom_call_target="tpu_custom_call" | custom-call | flops 6000000000 | bytes 8000000 | tf_op jit(solution)/shard_map/pallas_call | solution.py:414
  55.5 1.7 %copy.19 = f32[20,16,256]{2,1,0:T(8,128)} copy(f32[20,16,256]{2,1,0:T(8,128)} %bitcast.12) | data formatting | bytes 655360
  57.2 2.3 %copy.20 = f32[1,64,16,256]{3,2,1,0:T(8,128)} copy(f32[1,64,16,256]{3,2,1,0:T(8,128)} %bitcast.11) | data formatting | bytes 2097152

commit v4 on v3

--- a/solution.py
+++ b/solution.py
@@ -54,11 +54,9 @@
     a_high, a_low = pieces(across)
     r_high, r_low = pieces(rim)
     return (
-        z_high,
-        z_low,
-        np.concatenate([a_high, a_low], axis=0),
-        np.concatenate([r_high, r_high], axis=1),
-        r_low,
+        np.concatenate([z_high, z_high, z_low], axis=0),
+        np.concatenate([a_high, a_high, a_low], axis=1),
+        np.concatenate([r_high, r_high, r_low], axis=1),
     )
 
 
@@ -84,11 +82,9 @@
     codes,
     filter_hbm,
     offsets,
-    z_high_hbm,
-    z_low_hbm,
+    along_z_hbm,
     across_hbm,
-    rim_high_hbm,
-    rim_low_hbm,
+    rim_hbm,
     now_hbm,
     previous_hbm,
     velocity_hbm,
@@ -97,11 +93,9 @@
     last_hbm,
     residual,
     time_filter,
-    z_high,
-    z_low,
+    along_z,
     across,
-    rim_high,
-    rim_low,
+    rim_matrix,
     q,
     high,
     low,
@@ -134,11 +128,9 @@
         (now_hbm, q.at[0]),
         (residual_hbm, residual),
         (filter_hbm, time_filter),
-        (z_high_hbm, z_high),
-        (z_low_hbm, z_low),
+        (along_z_hbm, along_z),
         (across_hbm, across),
-        (rim_high_hbm, rim_high),
-        (rim_low_hbm, rim_low),
+        (rim_hbm, rim_matrix),
         (previous_hbm, q.at[1]),
         (velocity_hbm, speed),
         (forward_hbm, forward),
@@ -146,7 +138,7 @@
     loads = [
         pltpu.make_async_copy(there, here, local_sem.at[i]) for i, (there, here) in enumerate(pairs)
     ]
-    for load in loads:
+    for load in loads[:3]:
         load.start()
 
     barrier = pltpu.get_barrier_semaphore()
@@ -259,6 +251,8 @@
         low[slot, pl.ds(PAD + c * ROWS, ROWS), :] = value_low
 
     loads[0].wait()
+    for load in loads[3:]:
+        load.start()
     for c in range(chunks):
         publish_edges(0, c, q[0, pl.ds(c * ROWS, ROWS), :])
     loads[1].wait()
@@ -271,12 +265,14 @@
     for c in range(chunks):
         publish_pieces(0, c, q[0, pl.ds(c * ROWS, ROWS), :])
 
-    for d in range(1, spaces):
-        gather_arrival(d).wait_recv()
     first_cell = (me * cells).astype(F32)
 
-    def add_block(j, totals):
-        block = gathered[j]
+    def add_block(d, totals):
+        @pl.when(d > 0)
+        def _():
+            gather_arrival(d).wait_recv()
+
+        block = gathered[lax.rem(me + spaces - d, spaces)]
         block_high = block.astype(BF16).astype(F32)
         stacked = jnp.concatenate(
             [block_high, block - block_high, jnp.zeros((112, block.shape[1]), F32)], axis=0
@@ -292,7 +288,7 @@
     lax.fori_loop(0, spaces, add_block, 0)
     source[...] = source[...] + pltpu.roll(source[...], 120, 1)
 
-    for load in loads[3:]:
+    for load in loads[3:-1]:
         load.wait()
 
     first_lane = lax.broadcasted_iota(jnp.int32, (ROWS, 128), 1) == 0
@@ -304,13 +300,13 @@
             rows = pl.ds(c * ROWS, ROWS)
             mid_high = high[slot, pl.ds(PAD + c * ROWS, ROWS), :]
             mid_low = low[slot, pl.ds(PAD + c * ROWS, ROWS), :]
-            spread = dot(mid_high, z_high[...]) + dot(mid_high, z_low[...])
-            spread = spread + dot(mid_low, z_high[...])
+            spread = dot(jnp.concatenate([mid_high, mid_low, mid_high], axis=1), along_z[...])
             parts = []
             for sub in range(2):
                 window = pl.ds((2 * c + sub) * 128, 256)
-                both = dot(across[...], high[slot, window, :])
-                parts.append(both[:128] + both[128:] + dot(across[0:128], low[slot, window, :]))
+                near = high[slot, window, :]
+                stacked = jnp.concatenate([near, low[slot, window, :], near], axis=0)
+                parts.append(dot(across[...], stacked))
             spread = spread + jnp.concatenate(parts, axis=0)
 
             @pl.when(has_left)
@@ -324,8 +320,7 @@
             at = pl.ds(c * EDGE, EDGE)
             rim = jnp.concatenate([halo_in[slot, 0, at, :], halo_in[slot, 1, at, :]], axis=0)
             rim_h, rim_l = split(rim)
-            spread = spread + dot(rim_high[...], jnp.concatenate([rim_h, rim_l], axis=0))
-            spread = spread + dot(rim_low[...], rim_h)
+            spread = spread + dot(rim_matrix[...], jnp.concatenate([rim_h, rim_l, rim_h], axis=0))
 
             value = 2.0 * q[slot, rows, :] - q[other, rows, :] + speed[rows, :] * spread
             added = source[rows, :]
@@ -342,6 +337,12 @@
 
                 publish_edges(other, c, value)
                 publish_pieces(other, c, value)
+
+            if c == 0:
+
+                @pl.when(k == 0)
+                def _():
+                    loads[-1].wait()
 
             inside = pl.ds(lead + c * CHUNK_Y, CHUNK_Y)
             product = forward[k, rows, :].astype(F32) * value
@@ -417,7 +418,7 @@
             jax.ShapeDtypeStruct((band, depth), F32),
             jax.ShapeDtypeStruct((cells, depth), F32),
         ),
-        in_specs=[there, vmem, there, pl.BlockSpec(memory_space=pltpu.SMEM)] + [there] * 9,
+        in_specs=[there, vmem, there, pl.BlockSpec(memory_space=pltpu.SMEM)] + [there] * 7,
         out_specs=(vmem, pl.BlockSpec(memory_space=pl.ANY)),
         scratch_shapes=[
             pltpu.VMEM((records, residual.shape[2]), BF16),
@@ -435,7 +436,7 @@
             pltpu.VMEM((2, 2, chunks * EDGE, depth), F32),
             pltpu.VMEM((shots - 1, band, depth), F32),
             pltpu.VMEM((shots - 1, band, depth), F32),
-            pltpu.SemaphoreType.DMA((11,)),
+            pltpu.SemaphoreType.DMA((9,)),
             pltpu.SemaphoreType.DMA((spaces - 1,)),
             pltpu.SemaphoreType.DMA((spaces - 1,)),
             pltpu.SemaphoreType.DMA((2, 2, chunks)),

time: 59.7 us -> 58.2 us (0.975)
  Pallas kernels: 53 us -> 51.4 us
    pallas_call x1, Pallas kernels: 53 us -> 51.4 us  [local(): pl.pallas_call(functools.partial(kernel, spaces, shots, steps), out_shape...]
where the time goes in v4:
time: 58.2 us; the launch traced here: 57.9 us
  Pallas kernels  51.4 us (88%)
  local copies, waits for them, and re-layouts  3.98 us (7%)
  between operations  1.29 us (2%)
  other arithmetic  1.26 us (2%)
    pallas_call x1, Pallas kernels, local(): pl.pallas_call(functools.partial(kernel, spaces, shots, steps), out_shape...  51.4 us
    unnamed x2, local copies, waits for them, and re-layouts  3.98 us
    convert_element_type x1, other arithmetic, local(): codes = (record_tile[0, :, 0] * cells + record_cell[0]).astype(F32)[None]  1.26 us

profile of v4, /device:TPU:0, one launch (start us, length us, event | category | flops | bytes accessed | tf_op | source)
XLA Modules:
  0.0 57.9 jit_solution(17890533569873317450)
XLA Ops:
  1.3 1.3 %fusion.codes = f32[1,256]{1,0:T(1,128)} fusion(s32[1,256]{1,0:T(1,128)} %param.14, s32[1,256,1]{1,2,0:T(1,128)} %param.13), kind=kLoop, calls=%fused_computation.1 | loop fusion | flops 768 | bytes 3072 | tf_op jit(solution)/shard_map/convert_element_type | solution.py:411
  2.5 51.4 %shard_map.131 = (f32[320,256]{1,0:T(8,128)}, f32[1024,256]{1,0:T(8,128)}) custom-call(bf16[256,1536]{1,0:T(8,128)(2,1)} %bitcast.17, f32[1,256]{1,0:T(1,128)} %fusion.codes, bf16[6,1536]{1,0:T(8,128)(2,1)} %filter_hbm.1, s32[1]{0:T(128)S(6)} %copy.16.offsets, bf16[768,256]{1,0:T(8,128)(2,1)} %constant.8.clone.along_z_hbm, ...), custom_call_target="tpu_custom_call" | custom-call | flops 6000000000 | bytes 8000000 | tf_op jit(solution)/shard_map/pallas_call | solution.py:415
  54.0 1.7 %copy.17 = f32[20,16,256]{2,1,0:T(8,128)} copy(f32[20,16,256]{2,1,0:T(8,128)} %bitcast.12) | data formatting | bytes 655360
  55.7 2.3 %copy.18 = f32[1,64,16,256]{3,2,1,0:T(8,128)} copy(f32[1,64,16,256]{3,2,1,0:T(8,128)} %bitcast.11) | data formatting | bytes 2097152
